TPU v7x, 512 devices: a whole 4x8x8 slice. The times are simulated.
512 devices in a mesh: section: 16 (over y, x_hi), dp: 32 (over z, x_lo, core).
Axes of the slice: x: 4 (x_hi: 2, x_lo: 2; x = x_hi * 2 + x_lo), y: 8, z: 8, core: 2. Of those that a mesh axis runs over, the one named last changes fastest.
Arguments:
- saved_states: bfloat16 [16, 2, 128, 2688], P('section', None, 'dp'), may hold values from -64 to 64
- cotangent_in: bfloat16 [16, 128, 2688], P('section', 'dp'), may hold values from -6 to 6
- lengths: int32 [16], P('section'), may hold values from 16 to 128
- gain: bfloat16 [2688], replicated, may hold values from 0.099609375 to 1.8984375
- up_weight: bfloat16 [2688, 9216], P('section', 'dp'), may hold values from -0.125 to 0.125
- down_weight: bfloat16 [9216, 2688], P('dp', 'section'), may hold values from -0.0625 to 0.0625
Outputs:
- cotangent_out: bfloat16 [16, 128, 2688], P('section', 'dp')
- up_gradient: bfloat16 [2688, 9216], P('section', 'dp')
- down_gradient: bfloat16 [9216, 2688], P('dp', 'section')
- gain_gradient: float32 [2688], replicated
All inputs are finite; a program needn't handle non-finite values.
Results may differ from a plain program's by a relative error of at most 0.024.
Values may be sent and summed in bfloat16 or wider, within the bound.
A program may use at most 64 MiB of HBM per device.

v0:
```python
import math
import jax
import jax.numpy as jnp
from jax import lax
from jax.sharding import PartitionSpec as P

epsilon = 1e-06


def passed_along(block, axis, distance):
    devices = range(lax.axis_size(axis))
    route = [((i - distance) % len(devices), i) for i in devices]
    return lax.ppermute(block, axis, route)


def back_iteration(state, cotangent, gain, up_full, down_full):
    values = state.astype(jnp.float32)
    reciprocal = lax.rsqrt(jnp.mean(values * values, axis=-1, keepdims=True) + epsilon)
    scaled = values * reciprocal
    gain_wide = gain.astype(jnp.float32)
    normed = (scaled * gain_wide).astype(jnp.bfloat16)
    hidden_in = jnp.dot(normed, up_full, preferred_element_type=jnp.float32)
    sigma = jax.nn.sigmoid(hidden_in)
    hidden_out = (hidden_in * sigma).astype(jnp.bfloat16)
    back_out = lax.dot_general(
        cotangent, down_full, (((1,), (1,)), ((), ())), preferred_element_type=jnp.float32
    )
    back_in = (back_out * sigma * (1.0 + hidden_in * (1.0 - sigma))).astype(jnp.bfloat16)
    partial_value = lax.dot_general(
        back_in, up_full, (((1,), (1,)), ((), ())), preferred_element_type=jnp.float32
    )
    back_normed = lax.psum(partial_value.astype(jnp.bfloat16), "dp").astype(jnp.float32)
    rows_scaled, rows_recip, rows_cot = (scaled, reciprocal, cotangent)
    gained = back_normed * gain_wide
    back_state = rows_recip * (
        gained - rows_scaled * jnp.mean(gained * rows_scaled, axis=-1, keepdims=True)
    )
    result = (rows_cot.astype(jnp.float32) + back_state).astype(jnp.bfloat16)
    gain_term = jnp.sum(back_normed * rows_scaled, axis=0)
    return (result, normed, back_in, hidden_out, gain_term)


def hand_over(result):
    moved = passed_along(result, "section", -1)
    return moved


def contract_rows(left, right):
    return lax.dot_general(
        left, right, (((0,), (0,)), ((), ())), preferred_element_type=jnp.float32
    )


def reduce_terms(up_terms, down_terms):
    return (
        lax.psum_scatter(
            up_terms.astype(jnp.bfloat16), "section", scatter_dimension=0, tiled=True
        ).astype(jnp.float32),
        lax.psum_scatter(
            down_terms.astype(jnp.bfloat16), "section", scatter_dimension=1, tiled=True
        ).astype(jnp.float32),
    )


def on_device(saved_states, cotangent_in, lengths, gain, up_weight, down_weight):
    up_full, down_full = (
        lax.all_gather(up_weight, "section", axis=0, tiled=True),
        lax.all_gather(down_weight, "section", axis=1, tiled=True),
    )
    group_states, group_cotangent = (
        lax.all_gather(saved_states, "dp", axis=2, tiled=True),
        lax.all_gather(cotangent_in, "dp", axis=1, tiled=True),
    )
    turns = group_states.shape[1]
    tokens = group_states.shape[2]
    share = saved_states.shape[2]
    member = lax.axis_index("dp")
    positions = lax.broadcasted_iota(jnp.int32, (tokens, 1), 0)
    cotangent = jnp.where(
        positions < lengths[0], group_cotangent[0], jnp.zeros_like(group_cotangent[0])
    )
    scale = 1.0 / math.sqrt(turns * tokens * lax.axis_size("section"))
    gain_total = jnp.zeros((gain.shape[0],), jnp.float32)
    up_total = jnp.zeros(up_full.shape, jnp.float32)
    down_total = jnp.zeros(down_full.shape, jnp.float32)
    result = cotangent
    for turn in range(turns):
        if turn > 0:
            cotangent = hand_over(result)
        result, normed, back_in, hidden_out, gain_term = back_iteration(
            group_states[0, turn], cotangent, gain, up_full, down_full
        )
        gain_total = gain_total + gain_term
        up_total = up_total + contract_rows(normed, back_in)
        down_total = down_total + contract_rows(hidden_out, cotangent)
    up_sum, down_sum = reduce_terms(up_total * scale, down_total * scale)
    gain_sum = lax.psum(gain_total * scale, "section")
    own_rows = lax.dynamic_slice_in_dim(result, member * share, share, 0)[None]
    return (own_rows, up_sum.astype(jnp.bfloat16), down_sum.astype(jnp.bfloat16), gain_sum)


def solution(mesh):
    placed = (
        P("section", None, "dp", None),
        P("section", "dp", None),
        P("section"),
        P(),
        P("section", "dp"),
        P("dp", "section"),
    )
    return jax.shard_map(
        on_device,
        mesh=mesh,
        in_specs=placed,
        out_specs=(P("section", "dp", None), P("section", "dp"), P("dp", "section"), P()),
        check_vma=False,
    )
```

profile of v0, /device:TPU:16, one launch (start us, length us, event | category | flops | bytes accessed | tf_op | source)
XLA Modules:
  0.0 1156.4 jit_solution(15592596476500519794)
XLA Ops:
  7.2 0.0 all-gather.4.cloned.1.call-start
  7.2 1.4 copy.15
  8.6 0.0 all-gather.4.cloned.1.call-update
  8.7 0.0 all-gather.8.cloned.1.call-start
  8.7 0.7 all-gather.8.cloned.1.call-update
  9.4 0.0 all-gather.6.cloned.1.call-start
  9.5 0.7 all-gather.6.cloned.1.call-update
  10.2 0.0 all-reduce.5.cloned.1.call-start
  10.2 0.7 convert_element_type.71
  10.9 0.8 copy.14
  12.3 47.3 %all_gather.12 = bf16[1,128,2688]{2,0,1:T(2,128)(2,1)} all-gather(bf16[1,4,2688]{2,0,1:T(2,128)(2,1)S(1)} %copy.14), channel_id=1, replica_groups=mesh['section'=16,'dp'=32] {'dp'}, dimensions={1}, use_global_device_ids=true | all-gather | bytes 709632 | tf_op jit(solution)/shard_map/all_gather | solution.py:72
  59.6 22.9 %all-gather.4.cloned.1.call-done = bf16[1,2,128,2688]{3,1,0,2:T(2,128)(2,1)} async-done(((bf16[1,2,4,2688]{3,1,0,2:T(2,128)(2,1)}), bf16[1,2,128,2688]{3,1,0,2:T(2,128)(2,1)}) %all-gather.4.cloned.1.call-update) | async-done | bytes 1376272 | tf_op jit(solution)/shard_map/all_gather | solution.py:71
  82.5 5.2 fusion.36
  87.8 0.2 fusion.16
  88.0 86.3 %all-gather.8.cloned.1.call-done = bf16[2688,288]{1,0:T(8,128)(2,1)} async-done(((bf16[168,288]{1,0:T(8,128)(2,1)}), bf16[2688,288]{1,0:T(8,128)(2,1)}) %all-gather.8.cloned.1.call-update) | async-done | bytes 1548304 | tf_op jit(solution)/shard_map/all_gather | solution.py:67
  174.3 2.4 fusion.25
  176.7 0.0 copy-start.9
  176.7 0.0 copy-start
  176.7 88.4 %all-gather.6.cloned.1.call-done = bf16[288,2688]{0,1:T(8,128)(2,1)} async-done(((bf16[288,168]{0,1:T(8,128)(2,1)}), bf16[288,2688]{0,1:T(8,128)(2,1)}) %all-gather.6.cloned.1.call-update) | async-done | bytes 1548304 | tf_op jit(solution)/shard_map/all_gather | solution.py:68
  265.2 2.9 fusion.20
  268.0 0.0 copy-done.9
  268.0 0.0 copy-done
  268.0 0.0 copy-start.11
  268.1 1.7 convolution_convert_fusion.1
  269.7 0.0 copy-done.11
  269.7 0.0 all-reduce.5.cloned.1.call-update
  269.7 0.0 all-reduce.7.cloned.1.call-start
  269.8 224.5 %all-reduce.5.cloned.1.call-done = bf16[128,2688]{1,0:T(8,128)(2,1)} async-done(((bf16[128,2688]{1,0:T(8,128)(2,1)}), bf16[128,2688]{1,0:T(8,128)(2,1)}) %all-reduce.5.cloned.1.call-update) | async-done | bytes 688144 | tf_op jit(solution)/shard_map/psum | solution.py:32
  494.2 1.7 fusion.15
  496.0 0.0 copy-done.1
  496.0 0.0 copy-start.3
  496.0 1.7 fusion.11
  497.8 4.9 collective-permute-start
  502.6 0.0 copy-done.3
  502.6 0.2 fusion.17
  502.9 0.8 fusion.22
  503.8 0.0 copy-start.6
  503.8 14.3 %collective-permute-done = bf16[128,2688]{1,0:T(8,128)(2,1)S(1)} collective-permute-done((bf16[128,2688]{1,0:T(8,128)(2,1)S(1)}, bf16[128,2688]{1,0:T(8,128)(2,1)S(1)}, u32[]{:S(2)}, u32[]{:S(2)}) %collective-permute-start) | collective-permute-done | bytes 688160 | tf_op jit(solution)/shard_map/ppermute | solution.py:13
  518.1 0.0 copy-done.8
  518.1 0.8 fusion.21
  518.9 0.0 copy-done.6
  518.9 0.0 copy-done.4
  518.9 1.7 convolution_convert_fusion
  520.6 0.0 all-reduce.7.cloned.1.call-update
  520.6 0.0 reduce-scatter.7.cloned.1.call-start
  520.7 1.7 fusion.23
  522.4 2.2 fusion.2
  524.5 0.0 reduce-scatter.7.cloned.1.call-update
  524.6 0.0 copy-start.5
  524.6 0.0 copy-start.7
  524.6 0.2 reduce-scatter.9.cloned.1.call-start
  524.8 1.1 copy-done.2
  525.9 0.0 copy-done.10
  525.9 0.8 fusion.27
  526.7 2.1 fusion.3
  528.8 0.0 reduce-scatter.9.cloned.1.call-update
  528.8 0.1 dynamic-slice.5
  528.9 218.3 %all-reduce.7.cloned.1.call-done = bf16[128,2688]{1,0:T(8,128)(2,1)} async-done(((bf16[128,2688]{1,0:T(8,128)(2,1)}), bf16[128,2688]{1,0:T(8,128)(2,1)}) %all-reduce.7.cloned.1.call-update) | async-done | bytes 688144 | tf_op jit(solution)/shard_map/psum | solution.py:32
  747.2 2.5 fusion.12
  749.7 0.1 dynamic-slice.4
  749.8 72.7 %psum.23 = f32[2688]{0:T(1024)} all-reduce(f32[2688]{0:T(1024)S(1)} %add_multiply_fusion), channel_id=1, replica_groups=mesh['section'=16,'dp'=32] {'section'}, use_global_device_ids=true, to_apply=%region_10.11 | all-reduce | flops 2688 | bytes 21504 | tf_op jit(solution)/shard_map/psum | solution.py:97
  822.5 1.6 fusion.33
  824.1 125.8 %reduce-scatter.7.cloned.1.call-done = bf16[168,288]{1,0:T(8,128)(2,1)} async-done(((bf16[2688,288]{1,0:T(8,128)(2,1)}), bf16[168,288]{1,0:T(8,128)(2,1)}) %reduce-scatter.7.cloned.1.call-update) | async-done | bytes 96784
  949.9 199.7 %reduce-scatter.9.cloned.1.call-done = bf16[288,168]{0,1:T(8,128)(2,1)} async-done(((bf16[288,2688]{0,1:T(8,128)(2,1)}), bf16[288,168]{0,1:T(8,128)(2,1)}) %reduce-scatter.9.cloned.1.call-update) | async-done | bytes 96784
  (13 shorter events, 0.1 us)
Async XLA Ops:
  7.2 75.4 %all-gather.4.cloned.1.call-start = ((), (), s32[]{:S(2)}) async-start(), calls=%async_computation.2 | async-start | bytes 1419264 | tf_op jit(solution)/shard_map/all_gather | solution.py:71
  8.7 165.6 %all-gather.8.cloned.1.call-start = ((), (), s32[]{:S(2)}) async-start(), calls=%async_computation.4 | async-start | bytes 2193408 | tf_op jit(solution)/shard_map/all_gather | solution.py:67
  9.4 255.7 %all-gather.6.cloned.1.call-start = ((), (), s32[]{:S(2)}) async-start(), calls=%async_computation.3 | async-start | bytes 2193408 | tf_op jit(solution)/shard_map/all_gather | solution.py:68
  10.2 484.1 %all-reduce.5.cloned.1.call-start = ((), (), s32[]{:S(2)}) async-start(), calls=%async_computation.5 | async-start | bytes 1376256 | tf_op jit(solution)/shard_map/psum | solution.py:32
  176.7 91.3 %copy-start.9 = (f32[128,288]{0,1:T(8,128)}, f32[128,288]{0,1:T(8,128)S(1)}, u32[]{:S(2)}) copy-start(f32[128,288]{0,1:T(8,128)S(1)} %fusion.25) | copy-start | bytes 442372
  176.7 91.3 %copy-start = (bf16[2688,288]{1,0:T(8,128)(2,1)S(1)}, bf16[2688,288]{1,0:T(8,128)(2,1)}, u32[]{:S(2)}) copy-start(bf16[2688,288]{1,0:T(8,128)(2,1)} %all-gather.8.cloned.1.call-done) | copy-start | bytes 4644868
  268.0 1.7 copy-start.11
  269.7 477.4 %all-reduce.7.cloned.1.call-start = ((), (), s32[]{:S(2)}) async-start(), calls=%async_computation.6 | async-start | bytes 1376256 | tf_op jit(solution)/shard_map/psum | solution.py:32
  494.2 1.8 copy-start.1
  496.0 6.6 copy-start.3
  497.8 20.3 %collective-permute-start = (bf16[128,2688]{1,0:T(8,128)(2,1)S(1)}, bf16[128,2688]{1,0:T(8,128)(2,1)S(1)}, u32[]{:S(2)}, u32[]{:S(2)}) collective-permute-start(bf16[128,2688]{1,0:T(8,128)(2,1)S(1)} %fusion.11), channel_id=1, source_target_pairs={{32,0},{64,32},{96,64},{128,96},{160,128},{192,160},{224,192},{256... | collective-permute-start | bytes 2064392 | tf_op jit(solution)/shard_map/ppermute | solution.py:13
  502.9 15.2 %copy-start.8 = (bf16[288,2688]{0,1:T(8,128)(2,1)S(1)}, bf16[288,2688]{0,1:T(8,128)(2,1)}, u32[]{:S(2)}) copy-start(bf16[288,2688]{0,1:T(8,128)(2,1)} %all-gather.6.cloned.1.call-done) | copy-start | bytes 4644868
  503.8 15.1 %copy-start.6 = (f32[128,288]{0,1:T(8,128)}, f32[128,288]{0,1:T(8,128)S(1)}, u32[]{:S(2)}) copy-start(f32[128,288]{0,1:T(8,128)S(1)} %fusion.22) | copy-start | bytes 442372
  518.1 0.9 copy-start.4
  520.6 429.2 %reduce-scatter.7.cloned.1.call-start = ((), (), s32[]{:S(2)}) async-start(), calls=%async_computation.7 | async-start | bytes 2193408
  524.5 1.3 copy-start.2
  524.5 1.3 copy-start.10
  524.6 2.1 copy-start.5
  524.6 2.1 copy-start.7
  524.6 625.0 %reduce-scatter.9.cloned.1.call-start = ((), (), s32[]{:S(2)}) async-start(), calls=%async_computation.8 | async-start | bytes 2193408
Sparse Core Ops, SparseCore 0:
  10.7 71.7 all-gather.3
  85.7 88.5 all-gather.7
  177.5 87.6 all-gather.5
  269.9 224.3 all-reduce.4
  520.8 226.3 all-reduce.6
  752.1 197.6 reduce-scatter.6
  955.0 194.5 reduce-scatter.8
where the time goes:
time: 1160 us
  waiting for transfers between devices  982 us (85%)
  blocking collectives  120 us (10%)
  matrix products  17.1 us (1%)
  between operations  15 us (1%)
    psum x2, waiting for transfers between devices, back_iteration(): lax.psum(partial_value.astype(jnp.bfloat16), 'dp').astype(jnp.float32)  443 us
    unnamed x9, waiting for transfers between devices  327 us
    all_gather x1, waiting for transfers between devices, on_device(): lax.all_gather(down_weight, 'section', axis=1, tiled=True)  88.4 us
    all_gather x1, waiting for transfers between devices, on_device(): lax.all_gather(up_weight, 'section', axis=0, tiled=True)  86.3 us
    psum x1, blocking collectives, on_device(): gain_sum = lax.psum(gain_total * scale, 'section')  72.7 us
    all_gather x1, blocking collectives, on_device(): lax.all_gather(cotangent_in, 'dp', axis=1, tiled=True)  47.3 us
  transfers between devices with their start and end apart: 8, of which 8 were waited for; matrix products, arithmetic and copies ran while one was open for 2% of the time, Pallas kernels for 0%

commit v1 on v0

--- a/solution.py
+++ b/solution.py
@@ -5,6 +5,11 @@
 from jax.sharding import PartitionSpec as P
 
 epsilon = 1e-06
+
+
+def add_all(shard, axis):
+    blocks = lax.all_gather(shard, axis)
+    return jnp.sum(blocks, axis=0)
 
 
 def passed_along(block, axis, distance):
@@ -29,7 +34,7 @@
     partial_value = lax.dot_general(
         back_in, up_full, (((1,), (1,)), ((), ())), preferred_element_type=jnp.float32
     )
-    back_normed = lax.psum(partial_value.astype(jnp.bfloat16), "dp").astype(jnp.float32)
+    back_normed = add_all(partial_value.astype(jnp.bfloat16), "dp").astype(jnp.float32)
     rows_scaled, rows_recip, rows_cot = (scaled, reciprocal, cotangent)
     gained = back_normed * gain_wide
     back_state = rows_recip * (

time: 1160 us -> 975 us (0.84)
  waiting for transfers between devices: 982 us -> 777 us
  other arithmetic: 8.83 us -> 29.9 us
    psum x2 -> x0, waiting for transfers between devices: 443 us -> none  [back_iteration(): lax.psum(partial_value.astype(jnp.bfloat16), 'dp').astype(jnp.float32)]
    all_gather x0 -> x2, waiting for transfers between devices: none -> 250 us  [add_all(): blocks = lax.all_gather(shard, axis)]
    reduce_sum x0 -> x2, other arithmetic: none -> 24.5 us  [add_all(): return jnp.sum(blocks, axis=0)]
    unnamed x9, waiting for transfers between devices: 327 us -> 315 us
  transfers between devices with their start and end apart: 8 -> 8, of which waited for: 8 -> 8; matrix products, arithmetic and copies ran while one was open for 2% -> 3% of each run, Pallas kernels for 0% -> 0%
where the time goes in v1:
time: 975 us; the launch traced here: 974 us
  waiting for transfers between devices  777 us (80%)
  blocking collectives  120 us (12%)
  other arithmetic  29.9 us (3%)
  matrix products  17.8 us (2%)
  between operations  15 us (2%)
    unnamed x9, waiting for transfers between devices  315 us
    all_gather x2, waiting for transfers between devices, add_all(): blocks = lax.all_gather(shard, axis)  250 us
    all_gather x1, waiting for transfers between devices, on_device(): lax.all_gather(down_weight, 'section', axis=1, tiled=True)  88.4 us
    all_gather x1, waiting for transfers between devices, on_device(): lax.all_gather(up_weight, 'section', axis=0, tiled=True)  86.3 us
    psum x1, blocking collectives, on_device(): gain_sum = lax.psum(gain_total * scale, 'section')  73 us
    all_gather x1, blocking collectives, on_device(): lax.all_gather(cotangent_in, 'dp', axis=1, tiled=True)  47.2 us
    reduce_sum x2, other arithmetic, add_all(): return jnp.sum(blocks, axis=0)  24.5 us
    all_gather x1, waiting for transfers between devices, on_device(): lax.all_gather(saved_states, 'dp', axis=2, tiled=True)  23 us
  transfers between devices with their start and end apart: 8, of which 8 were waited for; matrix products, arithmetic and copies ran while one was open for 3% of the time, Pallas kernels for 0%

profile of v1, /device:TPU:16, one launch (start us, length us, event | category | flops | bytes accessed | tf_op | source)
XLA Modules:
  0.0 974.0 jit_solution(17856963264292540458)
XLA Ops:
  7.2 0.0 all-gather.8.cloned.1.call-start
  7.2 1.4 copy.15
  8.6 0.0 all-gather.8.cloned.1.call-update
  8.7 0.0 all-gather.12.cloned.1.call-start
  8.7 0.7 all-gather.12.cloned.1.call-update
  9.4 0.0 all-gather.10.cloned.1.call-start
  9.5 0.7 all-gather.10.cloned.1.call-update
  10.2 0.0 all-gather.14.cloned.1.call-start
  10.8 0.7 convert_element_type.75
  11.5 0.8 copy.14
  12.3 47.2 %all_gather.24 = bf16[1,128,2688]{2,0,1:T(2,128)(2,1)} all-gather(bf16[1,4,2688]{2,0,1:T(2,128)(2,1)S(1)} %copy.14), channel_id=1, replica_groups=mesh['section'=16,'dp'=32] {'dp'}, dimensions={1}, use_global_device_ids=true | all-gather | bytes 709632 | tf_op jit(solution)/shard_map/all_gather | solution.py:77
  59.5 23.0 %all-gather.8.cloned.1.call-done = bf16[1,2,128,2688]{3,1,0,2:T(2,128)(2,1)} async-done(((bf16[1,2,4,2688]{3,1,0,2:T(2,128)(2,1)}), bf16[1,2,128,2688]{3,1,0,2:T(2,128)(2,1)}) %all-gather.8.cloned.1.call-update) | async-done | bytes 1376272 | tf_op jit(solution)/shard_map/all_gather | solution.py:76
  82.5 5.2 fusion.36
  87.8 0.2 fusion.16
  88.0 86.3 %all-gather.12.cloned.1.call-done = bf16[2688,288]{1,0:T(8,128)(2,1)} async-done(((bf16[168,288]{1,0:T(8,128)(2,1)}), bf16[2688,288]{1,0:T(8,128)(2,1)}) %all-gather.12.cloned.1.call-update) | async-done | bytes 1548304 | tf_op jit(solution)/shard_map/all_gather | solution.py:72
  174.3 2.4 fusion.25
  176.7 0.0 copy-start.8
  176.7 0.0 copy-start
  176.7 88.4 %all-gather.10.cloned.1.call-done = bf16[288,2688]{0,1:T(8,128)(2,1)} async-done(((bf16[288,168]{0,1:T(8,128)(2,1)}), bf16[288,2688]{0,1:T(8,128)(2,1)}) %all-gather.10.cloned.1.call-update) | async-done | bytes 1548304 | tf_op jit(solution)/shard_map/all_gather | solution.py:73
  265.2 2.9 fusion.20
  268.0 0.0 copy-done.8
  268.0 0.0 copy-done
  268.0 0.0 copy-start.9
  268.1 1.7 convolution_convert_fusion.1
  269.7 0.0 copy-done.9
  269.7 0.0 all-gather.14.cloned.1.call-update
  269.8 0.0 all-gather.16.cloned.1.call-start
  269.8 127.6 %all-gather.14.cloned.1.call-done = bf16[4096,2688]{1,0:T(8,128)(2,1)} async-done(((bf16[128,2688]{1,0:T(8,128)(2,1)}), bf16[4096,2688]{1,0:T(8,128)(2,1)}) %all-gather.14.cloned.1.call-update) | async-done | bytes 22020112 | tf_op jit(solution)/shard_map/all_gather | solution.py:11
  397.4 12.3 %reduce_sum.79 = bf16[128,2688]{1,0:T(8,128)(2,1)S(1)} reduce(bf16[32,128,2688]{2,1,0:T(8,128)(2,1)} %bitcast.40, bf16[]{:T(256)} %constant.10.clone.1), dimensions={0}, to_apply=%region_1.2 | reduce | flops 10665984 | bytes 22708226 | tf_op jit(solution)/shard_map/reduce_sum | solution.py:12
  409.7 0.0 copy-start.1
  409.7 0.5 fusion.15
  410.2 0.8 copy-done.1
  411.0 0.6 fusion.11
  411.6 4.9 collective-permute-start
  416.5 0.0 copy-done.2
  416.5 0.2 fusion.17
  416.7 0.8 fusion.22
  417.6 0.0 copy-start.5
  417.6 15.0 %collective-permute-done = bf16[128,2688]{1,0:T(8,128)(2,1)S(1)} collective-permute-done((bf16[128,2688]{1,0:T(8,128)(2,1)S(1)}, bf16[128,2688]{1,0:T(8,128)(2,1)S(1)}, u32[]{:S(2)}, u32[]{:S(2)}) %collective-permute-start) | collective-permute-done | bytes 688160 | tf_op jit(solution)/shard_map/ppermute | solution.py:18
  432.6 0.0 copy-done.7
  432.6 0.8 fusion.21
  433.4 0.0 copy-done.5
  433.4 0.1 copy-done.3
  433.5 1.7 convolution_convert_fusion
  435.2 0.0 all-gather.16.cloned.1.call-update
  435.2 0.0 copy-start.4
  435.2 0.0 reduce-scatter.9.cloned.1.call-start
  435.3 2.3 fusion.27
  437.6 2.2 fusion.3
  439.8 0.0 reduce-scatter.9.cloned.1.call-update
  439.8 0.2 reduce-scatter.7.cloned.1.call-start
  440.0 0.6 copy-done.10
  440.6 0.8 fusion.23
  441.4 2.2 fusion.2
  443.6 0.0 reduce-scatter.7.cloned.1.call-update
  443.7 0.1 dynamic-slice.5
  443.7 121.9 %all-gather.16.cloned.1.call-done = bf16[4096,2688]{1,0:T(8,128)(2,1)} async-done(((bf16[128,2688]{1,0:T(8,128)(2,1)}), bf16[4096,2688]{1,0:T(8,128)(2,1)}) %all-gather.16.cloned.1.call-update) | async-done | bytes 22020112 | tf_op jit(solution)/shard_map/all_gather | solution.py:11
  565.7 12.3 %reduce_sum.82 = bf16[128,2688]{1,0:T(8,128)(2,1)S(1)} reduce(bf16[32,128,2688]{2,1,0:T(8,128)(2,1)} %bitcast.39, bf16[]{:T(256)} %constant.10.clone.1), dimensions={0}, to_apply=%region_4.5 | reduce | flops 10665984 | bytes 22708226 | tf_op jit(solution)/shard_map/reduce_sum | solution.py:12
  578.0 1.4 fusion.12
  579.4 0.1 dynamic-slice.4
  579.5 73.0 %psum.7 = f32[2688]{0:T(1024)} all-reduce(f32[2688]{0:T(1024)S(1)} %add_multiply_fusion), channel_id=1, replica_groups=mesh['section'=16,'dp'=32] {'section'}, use_global_device_ids=true, to_apply=%region_10.11 | all-reduce | flops 2688 | bytes 21504 | tf_op jit(solution)/shard_map/psum | solution.py:102
  652.5 1.6 fusion.33
  654.1 113.1 %reduce-scatter.9.cloned.1.call-done = bf16[288,168]{0,1:T(8,128)(2,1)} async-done(((bf16[288,2688]{0,1:T(8,128)(2,1)}), bf16[288,168]{0,1:T(8,128)(2,1)}) %reduce-scatter.9.cloned.1.call-update) | async-done | bytes 96784
  767.2 199.9 %reduce-scatter.7.cloned.1.call-done = bf16[168,288]{1,0:T(8,128)(2,1)} async-done(((bf16[2688,288]{1,0:T(8,128)(2,1)}), bf16[168,288]{1,0:T(8,128)(2,1)}) %reduce-scatter.7.cloned.1.call-update) | async-done | bytes 96784
  (13 shorter events, 0.1 us)
Async XLA Ops:
  7.2 75.4 %all-gather.8.cloned.1.call-start = ((), (), s32[]{:S(2)}) async-start(), calls=%async_computation.2 | async-start | bytes 1419264 | tf_op jit(solution)/shard_map/all_gather | solution.py:76
  8.7 165.6 %all-gather.12.cloned.1.call-start = ((), (), s32[]{:S(2)}) async-start(), calls=%async_computation.4 | async-start | bytes 2193408 | tf_op jit(solution)/shard_map/all_gather | solution.py:72
  9.4 255.7 %all-gather.10.cloned.1.call-start = ((), (), s32[]{:S(2)}) async-start(), calls=%async_computation.3 | async-start | bytes 2193408 | tf_op jit(solution)/shard_map/all_gather | solution.py:73
  10.2 387.3 %all-gather.14.cloned.1.call-start = ((), (), s32[]{:S(2)}) async-start(), calls=%async_computation.5 | async-start | bytes 22708224 | tf_op jit(solution)/shard_map/all_gather | solution.py:11
  176.7 91.3 %copy-start.8 = (f32[128,288]{0,1:T(8,128)}, f32[128,288]{0,1:T(8,128)S(1)}, u32[]{:S(2)}) copy-start(f32[128,288]{0,1:T(8,128)S(1)} %fusion.25) | copy-start | bytes 442372
  176.7 91.3 %copy-start = (bf16[2688,288]{1,0:T(8,128)(2,1)S(1)}, bf16[2688,288]{1,0:T(8,128)(2,1)}, u32[]{:S(2)}) copy-start(bf16[2688,288]{1,0:T(8,128)(2,1)} %all-gather.12.cloned.1.call-done) | copy-start | bytes 4644868
  268.0 1.7 copy-start.9
  269.8 295.9 %all-gather.16.cloned.1.call-start = ((), (), s32[]{:S(2)}) async-start(), calls=%async_computation.6 | async-start | bytes 22708224 | tf_op jit(solution)/shard_map/all_gather | solution.py:11
  409.7 1.3 copy-start.1
  411.0 5.4 copy-start.2
  411.6 21.0 %collective-permute-start = (bf16[128,2688]{1,0:T(8,128)(2,1)S(1)}, bf16[128,2688]{1,0:T(8,128)(2,1)S(1)}, u32[]{:S(2)}, u32[]{:S(2)}) collective-permute-start(bf16[128,2688]{1,0:T(8,128)(2,1)S(1)} %fusion.11), channel_id=1, source_target_pairs={{32,0},{64,32},{96,64},{128,96},{160,128},{192,160},{224,192},{256... | collective-permute-start | bytes 2064392 | tf_op jit(solution)/shard_map/ppermute | solution.py:18
  416.7 15.9 %copy-start.7 = (bf16[288,2688]{0,1:T(8,128)(2,1)S(1)}, bf16[288,2688]{0,1:T(8,128)(2,1)}, u32[]{:S(2)}) copy-start(bf16[288,2688]{0,1:T(8,128)(2,1)} %all-gather.10.cloned.1.call-done) | copy-start | bytes 4644868
  417.6 15.9 %copy-start.5 = (f32[128,288]{0,1:T(8,128)}, f32[128,288]{0,1:T(8,128)S(1)}, u32[]{:S(2)}) copy-start(f32[128,288]{0,1:T(8,128)S(1)} %fusion.22) | copy-start | bytes 442372
  432.6 0.9 copy-start.3
  435.2 2.4 copy-start.4
  435.2 2.4 copy-start.6
  435.2 332.0 %reduce-scatter.9.cloned.1.call-start = ((), (), s32[]{:S(2)}) async-start(), calls=%async_computation.8 | async-start | bytes 2193408
  439.8 0.9 copy-start.10
  439.8 527.3 %reduce-scatter.7.cloned.1.call-start = ((), (), s32[]{:S(2)}) async-start(), calls=%async_computation.7 | async-start | bytes 2193408
Sparse Core Ops, SparseCore 0:
  10.7 71.7 all-gather.7
  85.7 88.5 all-gather.11
  177.5 87.6 all-gather.9
  269.9 127.5 all-gather.13
  435.3 130.3 all-gather.15
  570.7 196.4 reduce-scatter.8
  772.3 194.7 reduce-scatter.6
